TPU v7x, 32 devices: a whole 2x2x4 slice. The times are simulated.
32 devices in a mesh: grp: 1, gx: 16 (over z, y, x), gy: 2 (over core).
Axes of the slice: x: 2, y: 2, z: 4, core: 2. Of those that a mesh axis runs over, the one named last changes fastest.
Arguments:
- field: bfloat16 [8, 256, 512, 256], P(None, ('grp', 'gx'), 'gy'), may hold values from -20 to 20, as said below
- factor_x_old: bfloat16 [256, 32], P(('grp', 'gx')), may hold values from -0.375 to 0.375
- factor_y_old: bfloat16 [512, 32], P(('grp', 'gy')), may hold values from -0.25 to 0.25
- factor_z: bfloat16 [256, 32], replicated, may hold values from -0.375 to 0.375
- factor_t: bfloat16 [8, 4], replicated, may hold values from -2 to 2
Outputs:
- factor_x: float32 [256, 32], P(('grp', 'gx'))
- factor_y: float32 [512, 32], P(('grp', 'gy'))
- core: float32 [4096, 32], P(('grp', 'gx', 'gy'))
Inputs may be any that keep to these rules, and one draw needn't show every extreme that they name: A field of order one whose magnitude varies across the grid.
All inputs are finite; a program needn't handle non-finite values.
Results may differ from a plain program's by a relative error of at most 0.002.
Values may be sent and summed in bfloat16 or wider, within the bound.
A program may use at most 64 MiB of HBM per device.

v0:
```python
import math

import jax
import jax.numpy as jnp
from jax import lax
from jax.sharding import PartitionSpec as P


def orthonormal(power, gram):
    lower = jnp.linalg.cholesky(gram)
    return jax.scipy.linalg.solve_triangular(lower, power.T, lower=True).T


def body(field, factor_x_old, factor_y_old, factor_z, factor_t):
    highest = lax.Precision.HIGHEST
    rows_x = field.shape[1]
    rank_x = factor_x_old.shape[1]
    rank_y = factor_y_old.shape[1]
    rank_z = factor_z.shape[1]
    rank_t = factor_t.shape[1]
    partial_q = jnp.einsum("txyz,zc->txcy", field, factor_z, preferred_element_type=jnp.float32)
    projected = jnp.einsum(
        "td,txcy->dxcy", factor_t.astype(jnp.float32), partial_q, precision=highest
    )
    local_rows = jnp.einsum(
        "dxcy,yb->xdcb", projected, factor_y_old.astype(jnp.float32), precision=highest
    )
    local_rows = local_rows.reshape(rows_x, rank_t * rank_z * rank_y)
    summed = lax.psum(local_rows, "gy")
    mode_rows = summed.astype(jnp.bfloat16)
    mode_float = mode_rows.astype(jnp.float32)
    gram = lax.dot_general(
        mode_rows,
        lax.all_gather(mode_rows, "gx", axis=0, tiled=True),
        (((1,), (1,)), ((), ())),
        preferred_element_type=jnp.float32,
    )
    power_x = jnp.dot(
        gram,
        lax.all_gather(factor_x_old, "gx", axis=0, tiled=True).astype(jnp.float32),
        precision=highest,
    )
    gram_x = lax.psum(jnp.dot(power_x.T, power_x, precision=highest), "gx")
    basis_x = orthonormal(power_x, gram_x)
    core_x = lax.psum(jnp.dot(basis_x.T, mode_float, precision=highest), "gx")
    spread = jnp.dot(basis_x, core_x, precision=highest).reshape(rows_x, rank_t, rank_z, rank_y)
    part_y = jnp.einsum("dxcy,xdcb->yb", projected, spread, precision=highest)
    power_y = lax.psum(part_y, "gx")
    gram_y = lax.psum(jnp.dot(power_y.T, power_y, precision=highest), "gy")
    basis_y = orthonormal(power_y, gram_y)
    folded = jnp.einsum("dxcy,yb->dxcb", projected, basis_y, precision=highest)
    core_term = jnp.einsum("dxcb,xa->dcab", folded, basis_x, precision=highest).reshape(
        rank_t * rank_z * rank_x, rank_y
    )
    core = lax.psum_scatter(core_term, ("gx", "gy"), scatter_dimension=0, tiled=True)
    total_x = rows_x * lax.axis_size("gx")
    total_y = power_y.shape[0] * lax.axis_size("gy")
    return (math.sqrt(total_x) * basis_x, math.sqrt(total_y) * basis_y, core)


def solution(mesh):
    placed = (
        P(None, ("grp", "gx"), "gy", None),
        P(("grp", "gx"), None),
        P(("grp", "gy"), None),
        P(),
        P(),
    )
    return jax.shard_map(
        body,
        mesh=mesh,
        in_specs=placed,
        out_specs=(P(("grp", "gx"), None), P(("grp", "gy"), None), P(("grp", "gx", "gy"), None)),
        check_vma=False,
    )
```

profile of v0, /device:TPU:0, one launch (start us, length us, event | category | flops | bytes accessed | tf_op | source)
XLA Modules:
  0.0 518.6 jit_solution(6829835584605686235)
XLA Ops:
  7.2 0.0 copy-start
  7.2 0.0 all-gather.2.cloned.1.call-start
  7.2 0.7 copy-done
  7.9 12.7 %fusion.23 = f32[32,8,16,256]{3,0,2,1:T(8,128)} fusion(bf16[8,16,256,256]{3,2,1,0:T(8,128)(2,1)} %param.6, bf16[256,32]{0,1:T(8,128)(2,1)S(1)} %copy-done), kind=kOutput, calls=%fused_computation.20 | convolution fusion | flops 536870912 | bytes 20987904 | tf_op jit(solution)/shard_map/txyz,zc->txcy/dot_general | solution.py:21
  20.5 0.0 copy-done.4
  20.6 6.5 %fusion.9 = f32[4,16,32,256]{3,0,2,1:T(4,128)S(1)} fusion(f32[32,8,16,256]{3,0,2,1:T(8,128)} %fusion.23, bf16[8,4]{0,1:T(4,128)(2,1)S(1)} %copy-done.4), kind=kOutput, calls=%fused_computation.9 | convolution fusion | flops 50331648 | bytes 6291520 | tf_op jit(solution)/shard_map/td,txcy->dxcy/dot_general | solution.py:22
  27.0 1.2 fusion.12
  28.3 0.0 copy-start.3
  28.3 0.1 copy.17
  28.4 0.5 reshape.28
  28.9 5.0 all-reduce.4
  33.8 0.0 all-gather.2.cloned.1.call-update
  33.9 0.0 all-reduce.3.cloned.1.call-start
  33.9 42.6 %all_gather.7 = bf16[256,32]{1,0:T(8,128)(2,1)S(1)} all-gather(bf16[16,32]{1,0:T(8,128)(2,1)S(1)} %copy-done.3), channel_id=1, replica_groups=mesh['grp'=1,'gx'=16,'gy'=2] {'gx'}, dimensions={0}, use_global_device_ids=true | all-gather | bytes 17408 | tf_op jit(solution)/shard_map/all_gather | solution.py:40
  76.5 20.8 %all-gather.2.cloned.1.call-done = bf16[256,4096]{1,0:T(8,128)(2,1)} async-done(((bf16[16,4096]{1,0:T(8,128)(2,1)}), bf16[256,4096]{1,0:T(8,128)(2,1)}) %all-gather.2.cloned.1.call-update) | async-done | bytes 2097168 | tf_op jit(solution)/shard_map/all_gather | solution.py:34
  97.3 2.3 fusion.34
  99.6 0.2 fusion.35
  99.8 0.2 fusion.36
  100.0 74.5 %psum.36 = f32[32,32]{0,1:T(8,128)S(1)} all-reduce(f32[32,32]{0,1:T(8,128)S(1)} %fusion.36), channel_id=1, replica_groups=mesh['grp'=1,'gx'=16,'gy'=2] {'gx'}, use_global_device_ids=true, to_apply=%region_1.0 | all-reduce | flops 1024 | bytes 8192 | tf_op jit(solution)/shard_map/psum | solution.py:43
  174.5 0.1 copy.19
  174.6 2.9 cholesky.44
  177.5 0.6 compare_reduce_fusion.1
  178.2 0.7 fusion.20
  178.8 2.5 custom-call.10
  181.3 0.1 fusion.28
  181.4 1.2 fusion.37
  182.6 0.0 all-reduce.3.cloned.1.call-update
  182.7 0.2 reduce-scatter.2.cloned.1.call-start
  182.9 104.1 %all-reduce.3.cloned.1.call-done = f32[32,4096]{1,0:T(8,128)} async-done(((f32[32,4096]{1,0:T(8,128)}), f32[32,4096]{1,0:T(8,128)}) %all-reduce.3.cloned.1.call-update) | async-done | bytes 524304 | tf_op jit(solution)/shard_map/psum | solution.py:45
  287.0 1.4 fusion.38
  288.4 0.3 reshape.29
  288.8 2.0 fusion.15
  290.8 74.8 %psum.38 = f32[256,32]{0,1:T(8,128)S(1)} all-reduce(f32[256,32]{0,1:T(8,128)S(1)} %fusion.15), channel_id=1, replica_groups=mesh['grp'=1,'gx'=16,'gy'=2] {'gx'}, use_global_device_ids=true, to_apply=%region_5.7 | all-reduce | flops 8192 | bytes 65536 | tf_op jit(solution)/shard_map/psum | solution.py:48
  365.6 0.2 fusion.39
  365.8 3.4 psum.39
  369.2 0.1 copy.23
  369.2 2.9 cholesky.55
  372.2 0.6 compare_reduce_fusion
  372.8 0.7 fusion.21
  373.5 2.5 custom-call.11
  376.0 0.2 fusion.25
  376.2 2.8 fusion.3
  378.9 1.8 fusion.31
  380.8 1.4 copy.24
  382.2 0.0 reduce-scatter.2.cloned.1.call-update
  382.2 0.6 multiply_bitcast_fusion.1
  382.8 0.6 multiply_bitcast_fusion
  383.4 128.7 %reduce-scatter.2.cloned.1.call-done = f32[128,32]{0,1:T(8,128)} async-done(((f32[4096,32]{0,1:T(8,128)}), f32[128,32]{0,1:T(8,128)}) %reduce-scatter.2.cloned.1.call-update) | async-done | bytes 16400 | tf_op jit(solution)/shard_map/reduce_scatter | solution.py:55
  (10 shorter events, 0.1 us)
Async XLA Ops:
  7.2 0.7 copy-start
  7.2 13.4 %copy-start.4 = (bf16[8,4]{0,1:T(4,128)(2,1)S(1)}, bf16[8,4]{0,1:T(4,128)(2,1)}, u32[]{:S(2)}) copy-start(bf16[8,4]{0,1:T(4,128)(2,1)} %param.10) | copy-start | bytes 196
  7.2 90.1 %all-gather.2.cloned.1.call-start = ((), (), s32[]{:S(2)}) async-start(), calls=%async_computation.1 | async-start | bytes 2228224 | tf_op jit(solution)/shard_map/all_gather | solution.py:34
  20.6 6.5 %copy-start.2 = (bf16[256,32]{0,1:T(8,128)(2,1)S(1)}, bf16[256,32]{0,1:T(8,128)(2,1)}, u32[]{:S(2)}) copy-start(bf16[256,32]{0,1:T(8,128)(2,1)} %param.8) | copy-start | bytes 49156
  28.3 5.6 %copy-start.3 = (bf16[16,32]{1,0:T(8,128)(2,1)S(1)}, bf16[16,32]{1,0:T(8,128)(2,1)}, u32[]{:S(2)}) copy-start(bf16[16,32]{1,0:T(8,128)(2,1)} %param.7) | copy-start | bytes 3076
  33.8 147.6 %copy-start.1 = (bf16[16,4096]{1,0:T(8,128)(2,1)S(1)}, bf16[16,4096]{1,0:T(8,128)(2,1)}, u32[]{:S(2)}) copy-start(bf16[16,4096]{1,0:T(8,128)(2,1)} %all-reduce.4) | copy-start | bytes 393220
  33.9 253.1 %all-reduce.3.cloned.1.call-start = ((), (), s32[]{:S(2)}) async-start(), calls=%async_computation.2 | async-start | bytes 1048576 | tf_op jit(solution)/shard_map/psum | solution.py:45
  182.7 329.5 %reduce-scatter.2.cloned.1.call-start = ((), (), s32[]{:S(2)}) async-start(), calls=%async_computation.3 | async-start | bytes 540672 | tf_op jit(solution)/shard_map/reduce_scatter | solution.py:55
Sparse Core Ops, SparseCore 0:
  34.0 63.2 all-gather.1
  182.8 104.1 all-reduce.2
  382.3 129.7 reduce-scatter.1
where the time goes:
time: 519 us
  waiting for transfers between devices  254 us (49%)
  blocking collectives  200 us (39%)
  matrix products  32.8 us (6%)
  other arithmetic  14.6 us (3%)
  between operations  13.9 us (3%)
    reduce_scatter x1, waiting for transfers between devices, body(): lax.psum_scatter(core_term, ('gx', 'gy'), scatter_dimension=0, tiled=True)  129 us
    psum x1, waiting for transfers between devices, body(): core_x = lax.psum(jnp.dot(basis_x.T, mode_float, precision=highest), 'gx')  104 us
    psum x1, blocking collectives, body(): power_y = lax.psum(part_y, 'gx')  74.8 us
    psum x1, blocking collectives, body(): gram_x = lax.psum(jnp.dot(power_x.T, power_x, precision=highest), 'gx')  74.5 us
    all_gather x1, blocking collectives, body(): lax.all_gather(factor_x_old, 'gx', axis=0, tiled=True).astype(jnp.float32)  42.6 us
    all_gather x1, waiting for transfers between devices, body(): lax.all_gather(mode_rows, 'gx', axis=0, tiled=True)  20.8 us
    dot_general x1, matrix products, body(): jnp.einsum('txyz,zc->txcy', field, factor_z, preferred_element_type=jnp.f...  12.7 us
  transfers between devices with their start and end apart: 3, of which 3 were waited for; matrix products, arithmetic and copies ran while one was open for 0% of the time, Pallas kernels for 0%

commit v1 on v0

--- a/solution.py
+++ b/solution.py
@@ -1,9 +1,342 @@
+import functools
 import math
 
 import jax
 import jax.numpy as jnp
 from jax import lax
+from jax.experimental import pallas as pl
+from jax.experimental.pallas import tpu as pltpu
 from jax.sharding import PartitionSpec as P
+
+MESH = pl.DeviceIdType.MESH
+HIGH = lax.Precision.HIGHEST
+F32 = jnp.float32
+BF16 = jnp.bfloat16
+LANES = 128
+NN = (((1,), (0,)), ((), ()))
+NT = (((1,), (1,)), ((), ()))
+TN = (((0,), (0,)), ((), ()))
+
+
+def mm(a, b, dims, precision=None):
+    return lax.dot_general(a, b, dims, precision=precision, preferred_element_type=F32)
+
+
+def split2(v):
+    hi = v.astype(BF16)
+    return hi, (v - hi.astype(F32)).astype(BF16)
+
+
+def split3(v):
+    hi = v.astype(BF16)
+    rest = v - hi.astype(F32)
+    mid = rest.astype(BF16)
+    return hi, mid, (rest - mid.astype(F32)).astype(BF16)
+
+
+def inverse_lower(gram):
+    n = gram.shape[0]
+    row = lax.broadcasted_iota(jnp.int32, (n, n), 0)
+    col = lax.broadcasted_iota(jnp.int32, (n, n), 1)
+    eye = jnp.where(row == col, 1.0, 0.0).astype(F32)
+    both = jnp.concatenate([gram, eye], axis=1)
+    at = lax.broadcasted_iota(jnp.int32, (n, 1), 0)
+    for j in range(n - 1):
+        pivot_row = both[j : j + 1, :]
+        scale = jnp.where(at > j, both[:, j : j + 1] / pivot_row[:, j : j + 1], 0.0)
+        both = both - scale * pivot_row
+    diag = jnp.sum(both[:, :n] * eye, axis=1, keepdims=True)
+    return both[:, n:] * lax.rsqrt(diag)
+
+
+def project_kernel(field_ref, fz_ref, ft_ref, fy_ref, pp_ref, a_ref, w_ref, fyt_ref):
+    steps = field_ref.shape[0]
+
+    @pl.when(pl.program_id(0) == 0)
+    def _():
+        for t in range(steps):
+            hi, lo = split2(fz_ref[...] * ft_ref[t : t + 1, :])
+            w_ref[t, :, :LANES] = hi
+            w_ref[t, :, LANES:] = lo
+        fyt_ref[...] = fy_ref[...].astype(F32).T.astype(BF16)
+
+    acc = mm(field_ref[0, 0], w_ref[0], NN)
+    for t in range(1, steps):
+        acc = acc + mm(field_ref[t, 0], w_ref[t], NN)
+    hi, lo = split2(acc[:, :LANES] + acc[:, LANES:])
+    pp = jnp.concatenate([hi, lo], axis=1)
+    pp_ref[0] = pp
+    rows = mm(fyt_ref[...], pp, NN)
+    a_ref[0] = rows[:, :LANES] + rows[:, LANES:]
+
+
+def tucker_kernel(
+    chips, scale_x, scale_y,
+    pp_ref, a_ref, fx_ref,
+    fx_out, fy_out, core_out,
+    part, other, y_all, qx_ref, s3, wy_send, wy_recv, my_send, my_recv, fold, fold2, shares, pair_in, mine, landed,
+    pair_sem, gather_send, gather_recv, give_send, give_recv, wy_sem, core_send, core_recv,
+):
+    grp = lax.axis_index("grp")
+    g = lax.axis_index("gx")
+    h = lax.axis_index("gy")
+    z = g // 4
+    p = g % 4
+    nx = a_ref.shape[0]
+    nb = a_ref.shape[1]
+    half = nb // 2 * LANES
+    xs = chips * nx
+    partner = (grp, g, 1 - h)
+
+    def peer(chip):
+        return (grp, chip, h)
+
+    barrier = pltpu.get_barrier_semaphore()
+    pl.semaphore_signal(barrier, inc=1, device_id=partner, device_id_type=MESH)
+    for k in range(1, chips):
+        pl.semaphore_signal(barrier, inc=1, device_id=peer((g + k) % chips), device_id_type=MESH)
+    for b in range(nb):
+        part[:, b * LANES : (b + 1) * LANES] = a_ref[:, b, :]
+    pl.semaphore_wait(barrier, chips)
+
+    swap = pltpu.make_async_remote_copy(
+        part, other, pair_sem.at[0], pair_sem.at[1], device_id=partner, device_id_type=MESH
+    )
+    swap.start()
+    own = pl.ds(pl.multiple_of(g * nx, nx), nx)
+    for s in range(2):
+        y_all[s, own, half:] = jnp.zeros((nx, LANES), BF16)
+        y_all[s, own, half : half + fx_ref.shape[1]] = fx_ref[...]
+    swap.wait()
+    for s in range(2):
+        at = slice(s * half, (s + 1) * half)
+        y_all[s, own, :half] = (part[:, at] + other[:, at]).astype(BF16)
+
+    def block(chip, side):
+        return y_all.at[side, pl.ds(pl.multiple_of(chip * nx, nx), nx), :]
+
+    def chip_of(q, k):
+        return ((z + 4 - k) % 4) * 4 + (p + q) % 4
+
+    def gather(q, k, target, source):
+        i = q * 4 + k
+        return pltpu.make_async_remote_copy(
+            block(source, h), block(source, h), gather_send.at[i], gather_recv.at[i],
+            device_id=peer(target), device_id_type=MESH,
+        )
+
+    def give(q, k):
+        i = q * 4 + k
+        source = chip_of(q, k)
+        return pltpu.make_async_remote_copy(
+            block(source, h), block(source, h), give_send.at[i], give_recv.at[i],
+            device_id=partner, device_id_type=MESH,
+        )
+
+    started = []
+    for k in (1, 3, 2):
+        c = gather(0, k, ((z + k) % 4) * 4 + p, g)
+        c.start()
+        started.append(c)
+    for q in (1, 3, 2):
+        c = gather(q, 0, z * 4 + (p + 4 - q) % 4, g)
+        c.start()
+        started.append(c)
+    gives = []
+
+    def arrived(q, k):
+        i = q * 4 + k
+        source = chip_of(q, k)
+        pltpu.make_async_remote_copy(
+            block(source, h), block(source, h), gather_send.at[i], gather_recv.at[i],
+            device_id=partner, device_id_type=MESH,
+        ).wait_recv()
+        c = give(q, k)
+        c.start()
+        gives.append((c, q, k))
+
+    for k in (1, 3, 2):
+        arrived(0, k)
+        for q in (1, 3, 2):
+            c = gather(q, k, z * 4 + (p + 4 - q) % 4, chip_of(0, k))
+            c.start()
+            started.append(c)
+    for k in (0, 1, 3, 2):
+        for q in (1, 3, 2):
+            arrived(q, k)
+    for c, q, k in gives:
+        i = q * 4 + k
+        theirs = block(chip_of(q, k), 1 - h)
+        pltpu.make_async_remote_copy(
+            theirs, theirs, give_send.at[i], give_recv.at[i], device_id=partner, device_id_type=MESH
+        ).wait_recv()
+    for c in started:
+        c.wait_send()
+    for c, q, k in gives:
+        c.wait_send()
+
+    left = y_all[0, :, :half]
+    right = y_all[1, :, :half]
+    gram = mm(left, left, NT) + mm(right, right, NT)
+    old = y_all[0, :, half:][:, : fx_ref.shape[1]].astype(F32)
+    power_x = mm(gram, old, NN, HIGH)
+    inv_x = inverse_lower(mm(power_x, power_x, TN, HIGH))
+    qx = mm(power_x, inv_x, NT, HIGH)
+    qx_ref[...] = qx
+    q_own = qx_ref[own, :]
+    fx_out[...] = scale_x * q_own
+    onto = jnp.concatenate(split3(mm(q_own, qx, NT, HIGH)), axis=0)
+    for s in range(2):
+        spread = mm(onto, y_all[s, :, :half], NN)
+        spread = spread[:nx] + spread[nx : 2 * nx] + spread[2 * nx :]
+        for b in range(nb // 2):
+            s3[s * (nb // 2) + b] = spread[:, b * LANES : (b + 1) * LANES]
+
+    acc = jnp.zeros((2 * nb, pp_ref.shape[1]), F32)
+    for x in range(nx):
+        hi, lo = split2(s3[:, x, :])
+        both = jnp.concatenate([jnp.concatenate([hi, hi], 1), jnp.concatenate([lo, lo], 1)], 0)
+        acc = acc + mm(both, pp_ref[x], NT)
+    power_y = acc[:nb] + acc[nb:]
+    for i, flip in enumerate((1, 2, 4, 8)):
+        low = g % (2 * flip)
+        target = jnp.where(low < flip, g + flip, g - flip)
+        wy_send[i] = power_y
+        c = pltpu.make_async_remote_copy(
+            wy_send.at[i], wy_recv.at[i], wy_sem.at[0, i], wy_sem.at[1, i],
+            device_id=peer(target), device_id_type=MESH,
+        )
+        c.start()
+        c.wait()
+        power_y = power_y + wy_recv[i]
+
+    my_send[...] = jnp.zeros(my_send.shape, F32)
+    my_send[:, :nb] = mm(power_y, power_y, NT, HIGH)
+    my_copy = pltpu.make_async_remote_copy(
+        my_send, my_recv, pair_sem.at[2], pair_sem.at[3], device_id=partner, device_id_type=MESH
+    )
+    my_copy.start()
+
+    wy2 = jnp.concatenate(split2(power_y), axis=0)
+    for x in range(nx):
+        f = mm(wy2, pp_ref[x], NN)
+        f = f[:nb] + f[nb:]
+        fold[x] = f[:, :LANES] + f[:, LANES:]
+    for b in range(nb):
+        fold2[:, b * LANES : (b + 1) * LANES] = fold[:, b, :]
+    term = mm(q_own, fold2[...], TN, HIGH)
+    for r in range(8):
+        rows = jnp.concatenate(
+            [term[:, (u * 8 + r) * LANES : (u * 8 + r + 1) * LANES] for u in range(nb // 8)], axis=0
+        )
+        shares[:, r, :] = rows.T
+    mine_rows = shares.shape[0] // (2 * chips)
+    pair_copies = []
+    for c in range(chips):
+        src = shares.at[pl.ds((c * 2 + 1 - h) * mine_rows, mine_rows)]
+        cp = pltpu.make_async_remote_copy(
+            src, pair_in.at[c], core_send.at[0, c], core_recv.at[0, c],
+            device_id=partner, device_id_type=MESH,
+        )
+        cp.start()
+        pair_copies.append(cp)
+    for cp in pair_copies:
+        cp.wait()
+    for c in range(chips):
+        mine[c] = shares[pl.ds((c * 2 + h) * mine_rows, mine_rows)] + pair_in[c]
+    sends = []
+    for k in range(1, chips):
+        target = (g + k) % chips
+        cp = pltpu.make_async_remote_copy(
+            mine.at[target], landed.at[k], core_send.at[1, k], core_recv.at[1, k],
+            device_id=peer(target), device_id_type=MESH,
+        )
+        cp.start()
+        sends.append(cp)
+
+    my_copy.wait()
+    inv_y = inverse_lower(my_send[:, :nb] + my_recv[:, :nb])
+    fy_out[...] = scale_y * mm(power_y, inv_y, (((0,), (1,)), ((), ())), HIGH)
+
+    for cp in sends:
+        cp.wait()
+    total = mine[g]
+    for k in range(1, chips):
+        total = total + landed[k]
+    ra = fx_ref.shape[1]
+    columns = [
+        jnp.concatenate([total[i][:, u * ra : (u + 1) * ra] for u in range(nb // 8)], axis=0)
+        for i in range(mine_rows)
+    ]
+    raw = jnp.concatenate(columns, axis=1)
+    core_out[...] = mm(raw, inv_y, (((0,), (1,)), ((), ())), HIGH)
+
+
+def fast_body(chips, field, factor_x_old, factor_y_old, factor_z, factor_t):
+    nt, nx, ny, nz = field.shape
+    ra = factor_x_old.shape[1]
+    nb = factor_y_old.shape[1]
+    nc = factor_z.shape[1]
+    nd = factor_t.shape[1]
+    fz = jnp.tile(factor_z.astype(F32), (1, nd))
+    ft = jnp.repeat(factor_t.astype(F32), nc, axis=1)
+    whole = lambda shape: pl.BlockSpec(shape, lambda x: (0,) * len(shape))
+    pp, a = pl.pallas_call(
+        project_kernel,
+        grid=(nx,),
+        in_specs=[
+            pl.BlockSpec((nt, 1, ny, nz), lambda x: (0, x, 0, 0)),
+            whole((nz, LANES)), whole((nt, LANES)), whole((ny, nb)),
+        ],
+        out_specs=[
+            pl.BlockSpec((1, ny, 2 * LANES), lambda x: (x, 0, 0)),
+            pl.BlockSpec((1, nb, LANES), lambda x: (x, 0, 0)),
+        ],
+        out_shape=[
+            jax.ShapeDtypeStruct((nx, ny, 2 * LANES), BF16),
+            jax.ShapeDtypeStruct((nx, nb, LANES), F32),
+        ],
+        scratch_shapes=[pltpu.VMEM((nt, nz, 2 * LANES), BF16), pltpu.VMEM((nb, ny), BF16)],
+        compiler_params=pltpu.CompilerParams(
+            dimension_semantics=("arbitrary",), vmem_limit_bytes=32 << 20
+        ),
+    )(field, fz, ft, factor_y_old)
+    xs = nx * chips
+    wide = nb * LANES
+    rows = LANES // (2 * chips)
+    vmem = pl.BlockSpec(memory_space=pltpu.VMEM)
+    dma = pltpu.SemaphoreType.DMA
+    return pl.pallas_call(
+        functools.partial(tucker_kernel, chips, math.sqrt(xs), math.sqrt(2 * ny)),
+        in_specs=[vmem] * 3,
+        out_specs=[vmem] * 3,
+        out_shape=[
+            jax.ShapeDtypeStruct((nx, ra), F32),
+            jax.ShapeDtypeStruct((ny, nb), F32),
+            jax.ShapeDtypeStruct((rows * ra, nb), F32),
+        ],
+        scratch_shapes=[
+            pltpu.VMEM((nx, wide), F32),
+            pltpu.VMEM((nx, wide), F32),
+            pltpu.VMEM((2, xs, wide // 2 + LANES), BF16),
+            pltpu.VMEM((xs, ra), F32),
+            pltpu.VMEM((nb, nx, LANES), F32),
+            pltpu.VMEM((4, nb, ny), F32),
+            pltpu.VMEM((4, nb, ny), F32),
+            pltpu.VMEM((nb, LANES), F32),
+            pltpu.VMEM((nb, LANES), F32),
+            pltpu.VMEM((nx, nb, LANES), F32),
+            pltpu.VMEM((nx, wide), F32),
+            pltpu.VMEM((LANES, 8, LANES), F32),
+            pltpu.VMEM((chips, rows, 8, LANES), F32),
+            pltpu.VMEM((chips, rows, 8, LANES), F32),
+            pltpu.VMEM((chips, rows, 8, LANES), F32),
+            dma((4,)), dma((16,)), dma((16,)), dma((16,)), dma((16,)), dma((2, 4)), dma((2, chips)), dma((2, chips)),
+        ],
+        compiler_params=pltpu.CompilerParams(
+            collective_id=0, has_side_effects=True, vmem_limit_bytes=40 << 20
+        ),
+    )(pp, a, factor_x_old)
 
 
 def orthonormal(power, gram):
@@ -66,8 +399,26 @@
         P(),
         P(),
     )
+    chips = mesh.shape["gx"]
+
+    def run(field, factor_x_old, factor_y_old, factor_z, factor_t):
+        packed = factor_z.shape[1] * factor_t.shape[1]
+        fits = (
+            chips == 16
+            and mesh.shape["gy"] == 2
+            and packed == LANES
+            and field.shape[1] == 16
+            and factor_x_old.shape[1] == 32
+            and factor_y_old.shape[1] == 32
+            and field.shape[2] % 256 == 0
+            and field.shape[3] % 256 == 0
+        )
+        if fits:
+            return fast_body(chips, field, factor_x_old, factor_y_old, factor_z, factor_t)
+        return body(field, factor_x_old, factor_y_old, factor_z, factor_t)
+
     return jax.shard_map(
-        body,
+        run,
         mesh=mesh,
         in_specs=placed,
         out_specs=(P(("grp", "gx"), None), P(("grp", "gy"), None), P(("grp", "gx", "gy"), None)),

time: 519 us -> 76.4 us (0.15)
  waiting for transfers between devices: 254 us -> 0 us
  blocking collectives: 200 us -> 0 us
  Pallas kernels: 0 us -> 65.1 us
  matrix products: 32.8 us -> 0 us
  other arithmetic: 14.6 us -> 0 us
  between operations: 13.9 us -> 0.67 us
  local copies, waits for them, and re-layouts: 3.11 us -> 10.3 us
    psum x4 -> x0, blocking collectives: 158 us -> none  [the longest x1 74.8 us: body(): power_y = lax.psum(part_y, 'gx')]
    reduce_scatter x1 -> x0, waiting for transfers between devices: 129 us -> none  [body(): lax.psum_scatter(core_term, ('gx', 'gy'), scatter_dimension=0, tiled=True)]
    psum x1 -> x0, waiting for transfers between devices: 104 us -> none  [body(): core_x = lax.psum(jnp.dot(basis_x.T, mode_float, precision=highest), 'gx')]
    pallas_call x0 -> x2, Pallas kernels: none -> 65.1 us  [the longest x1 54 us: fast_body(): pl.pallas_call(functools.partial(tucker_kernel, chips, math.sqrt(xs), mat...]
    all_gather x1 -> x0, blocking collectives: 42.6 us -> none  [body(): lax.all_gather(factor_x_old, 'gx', axis=0, tiled=True).astype(jnp.float32)]
    dot_general x12 -> x0, matrix products: 32.5 us -> none  [the longest x1 12.7 us: body(): jnp.einsum('txyz,zc->txcy', field, factor_z, preferred_element_type=jnp.f...]
    all_gather x1 -> x0, waiting for transfers between devices: 20.8 us -> none  [body(): lax.all_gather(mode_rows, 'gx', axis=0, tiled=True)]
    another operation x10 -> x0, other arithmetic: 13.4 us -> none  [the longest x6 7.19 us: orthonormal(): lower = jnp.linalg.cholesky(gram)]
  transfers between devices with their start and end apart: 3 -> 0, of which waited for: 3 -> 0; matrix products, arithmetic and copies ran while one was open for 0% -> 0% of each run, Pallas kernels for 0% -> 0%
where the time goes in v1:
time: 76.4 us; the launch traced here: 76.1 us
  Pallas kernels  65.1 us (85%)
  local copies, waits for them, and re-layouts  10.3 us (13%)
    pallas_call x1, Pallas kernels, fast_body(): pl.pallas_call(functools.partial(tucker_kernel, chips, math.sqrt(xs), mat...  54 us
    pallas_call x1, Pallas kernels, fast_body(): pl.pallas_call(project_kernel, grid=(nx,), in_specs=[pl.BlockSpec((nt, 1,...  11.1 us
    unnamed x6, local copies, waits for them, and re-layouts  7.21 us

profile of v1, /device:TPU:0, one launch (start us, length us, event | category | flops | bytes accessed | tf_op | source)
XLA Modules:
  0.0 76.1 jit_solution(9831561250394192805)
XLA Ops:
  0.6 0.0 copy-start.1
  0.6 0.8 %copy.13 = f32[8,4]{1,0:T(8,128)S(1)} copy(bf16[8,4]{0,1:T(4,128)(2,1)} %param.9) | data formatting | bytes 192 | tf_op jit(solution)/shard_map/convert_element_type | solution.py:282
  1.4 0.1 broadcast_in_dim.3
  1.5 0.1 reshape.13.ft_ref
  1.6 0.8 %copy.15.fy_ref = bf16[256,32]{1,0:T(8,128)(2,1)S(1)} copy(bf16[256,32]{0,1:T(8,128)(2,1)} %param.7) | data formatting | bytes 32768 | tf_op args[2]
  2.4 0.7 tile.4
  3.1 0.1 copy.14.fz_ref
  3.2 0.0 copy-start
  3.2 5.8 %copy-done = bf16[8,16,256,256]{3,2,1,0:T(8,128)(2,1)S(1)} copy-done((bf16[8,16,256,256]{3,2,1,0:T(8,128)(2,1)S(1)}, bf16[8,16,256,256]{3,2,1,0:T(8,128)(2,1)}, u32[]{:S(2)}) %copy-start) | copy-done | bytes 16777240
  9.0 11.1 %shard_map.76 = (bf16[16,256,256]{2,1,0:T(8,128)(2,1)S(1)}, f32[16,32,128]{2,1,0:T(8,128)S(1)}) custom-call(bf16[8,16,256,256]{3,2,1,0:T(8,128)(2,1)S(1)} %copy-done, f32[256,128]{1,0:T(8,128)S(1)} %copy.14.fz_ref, f32[8,128]{1,0:T(8,128)S(1)} %reshape.13.ft_ref, bf16[256,32]{1,0:T(8,128)(2,1)S(1)} %copy.15.fy_ref), custom_call_target="tpu_custom_call" | custom-call | tf_op jit(solution)/shard_map/pallas_call | solution.py:284
  20.1 0.0 copy-done.1
  20.1 54.0 %shard_map.77 = (f32[16,32]{1,0:T(8,128)S(1)}, f32[256,32]{1,0:T(8,128)S(1)}, f32[128,32]{1,0:T(8,128)S(1)}) custom-call(bf16[16,256,256]{2,1,0:T(8,128)(2,1)S(1)} %get-tuple-element.5.pp_ref, f32[16,32,128]{2,1,0:T(8,128)S(1)} %get-tuple-element.6.a_ref, bf16[16,32]{1,0:T(8,128)(2,1)S(1)} %copy-done.1), custom_call_target="tpu_custom_call" | custom-call | tf_op jit(solution)/shard_map/pallas_call | solution.py:309
  74.1 0.7 copy.17
  74.8 0.7 copy.16
  75.5 0.6 copy.19
Async XLA Ops:
  0.6 19.4 %copy-start.1 = (bf16[16,32]{1,0:T(8,128)(2,1)S(1)}, bf16[16,32]{1,0:T(8,128)(2,1)}, u32[]{:S(2)}) copy-start(bf16[16,32]{1,0:T(8,128)(2,1)} %fx_ref.1) | copy-start | bytes 3076
  3.2 5.8 %copy-start = (bf16[8,16,256,256]{3,2,1,0:T(8,128)(2,1)S(1)}, bf16[8,16,256,256]{3,2,1,0:T(8,128)(2,1)}, u32[]{:S(2)}) copy-start(bf16[8,16,256,256]{3,2,1,0:T(8,128)(2,1)} %field_ref.1) | copy-start | bytes 50331652

commit v2 on v1

--- a/solution.py
+++ b/solution.py
@@ -49,52 +49,70 @@
     return both[:, n:] * lax.rsqrt(diag)
 
 
-def project_kernel(field_ref, fz_ref, ft_ref, fy_ref, pp_ref, a_ref, w_ref, fyt_ref):
-    steps = field_ref.shape[0]
-
-    @pl.when(pl.program_id(0) == 0)
-    def _():
-        for t in range(steps):
-            hi, lo = split2(fz_ref[...] * ft_ref[t : t + 1, :])
-            w_ref[t, :, :LANES] = hi
-            w_ref[t, :, LANES:] = lo
-        fyt_ref[...] = fy_ref[...].astype(F32).T.astype(BF16)
-
-    acc = mm(field_ref[0, 0], w_ref[0], NN)
-    for t in range(1, steps):
-        acc = acc + mm(field_ref[t, 0], w_ref[t], NN)
-    hi, lo = split2(acc[:, :LANES] + acc[:, LANES:])
-    pp = jnp.concatenate([hi, lo], axis=1)
-    pp_ref[0] = pp
-    rows = mm(fyt_ref[...], pp, NN)
-    a_ref[0] = rows[:, :LANES] + rows[:, LANES:]
-
-
 def tucker_kernel(
     chips, scale_x, scale_y,
-    pp_ref, a_ref, fx_ref,
+    field_ref, fx_ref, fyt_ref, fzt_ref, ftt_ref,
     fx_out, fy_out, core_out,
-    part, other, y_all, qx_ref, s3, wy_send, wy_recv, my_send, my_recv, fold, fold2, shares, pair_in, mine, landed,
-    pair_sem, gather_send, gather_recv, give_send, give_recv, wy_sem, core_send, core_recv,
+    slots, w_ref, pp_ref, a_ref,
+    part, other, y_all, qx_ref, s3, wy_send, wy_recv, wy_all, my_send, my_recv, fold, fold2, shares, pair_in, mine, landed,
+    field_sem, pair_sem, gather_send, gather_recv, give_send, give_recv, wy_sem, core_send, core_recv,
 ):
     grp = lax.axis_index("grp")
     g = lax.axis_index("gx")
     h = lax.axis_index("gy")
     z = g // 4
     p = g % 4
-    nx = a_ref.shape[0]
-    nb = a_ref.shape[1]
+    depth, pair = slots.shape[0], slots.shape[2]
+    nt, nx = field_ref.shape[:2]
+    nb, ra, nd = fyt_ref.shape[0], fx_ref.shape[1], ftt_ref.shape[0]
+    nc = fzt_ref.shape[0]
     half = nb // 2 * LANES
-    xs = chips * nx
     partner = (grp, g, 1 - h)
 
     def peer(chip):
         return (grp, chip, h)
 
+    def fetch(i):
+        slot = lax.rem(i, depth)
+        return pltpu.make_async_copy(
+            field_ref.at[:, pl.ds(i * pair, pair)], slots.at[slot], field_sem.at[slot]
+        )
+
+    steps = nx // pair
+    for i in range(depth - 1):
+        fetch(i).start()
+
     barrier = pltpu.get_barrier_semaphore()
     pl.semaphore_signal(barrier, inc=1, device_id=partner, device_id_type=MESH)
     for k in range(1, chips):
         pl.semaphore_signal(barrier, inc=1, device_id=peer((g + k) % chips), device_id_type=MESH)
+
+    ftt = ftt_ref[...].astype(F32)
+    fz = jnp.concatenate([fzt_ref[...].astype(F32)] * nd, axis=0).T
+    ft = jnp.concatenate([jnp.broadcast_to(ftt[d : d + 1, :], (nc, nt)) for d in range(nd)], axis=0).T
+    for t in range(nt):
+        hi, lo = split2(fz * ft[t : t + 1, :])
+        w_ref[t, :, :LANES] = hi
+        w_ref[t, :, LANES:] = lo
+
+    @pl.loop(0, steps)
+    def _(i):
+        @pl.when(i + depth - 1 < steps)
+        def _():
+            fetch(i + depth - 1).start()
+
+        fetch(i).wait()
+        slot = lax.rem(i, depth)
+        for u in range(pair):
+            acc = mm(slots[slot, 0, u], w_ref[0], NN)
+            for t in range(1, nt):
+                acc = acc + mm(slots[slot, t, u], w_ref[t], NN)
+            hi, lo = split2(acc[:, :LANES] + acc[:, LANES:])
+            pp = jnp.concatenate([hi, lo], axis=1)
+            pp_ref[i * pair + u] = pp
+            rows = mm(fyt_ref[...], pp, NN)
+            a_ref[i * pair + u] = rows[:, :LANES] + rows[:, LANES:]
+
     for b in range(nb):
         part[:, b * LANES : (b + 1) * LANES] = a_ref[:, b, :]
     pl.semaphore_wait(barrier, chips)
@@ -106,79 +124,84 @@
     own = pl.ds(pl.multiple_of(g * nx, nx), nx)
     for s in range(2):
         y_all[s, own, half:] = jnp.zeros((nx, LANES), BF16)
-        y_all[s, own, half : half + fx_ref.shape[1]] = fx_ref[...]
+        y_all[s, own, half : half + ra] = fx_ref[...]
     swap.wait()
     for s in range(2):
         at = slice(s * half, (s + 1) * half)
         y_all[s, own, :half] = (part[:, at] + other[:, at]).astype(BF16)
 
-    def block(chip, side):
-        return y_all.at[side, pl.ds(pl.multiple_of(chip * nx, nx), nx), :]
+    along_x = p + 1 - 2 * (p % 2)
+    along_y = (p + 2) % 4
+    across = 3 - p
+    planes = (p, along_x, along_y, across)
+    columns = (slice(0, half + LANES), slice(0, half // 2), slice(half // 2, half + LANES))
 
     def chip_of(q, k):
-        return ((z + 4 - k) % 4) * 4 + (p + q) % 4
-
-    def gather(q, k, target, source):
-        i = q * 4 + k
+        return ((z + 4 - k) % 4) * 4 + planes[q]
+
+    def block(chip, side, cut):
+        return y_all.at[side, pl.ds(pl.multiple_of(chip * nx, nx), nx), columns[cut]]
+
+    def move(sems, q, k, cut, chip, side, target):
+        i = q * 4 + k + (4 if cut == 2 else 0)
+        ref = block(chip, side, cut)
         return pltpu.make_async_remote_copy(
-            block(source, h), block(source, h), gather_send.at[i], gather_recv.at[i],
-            device_id=peer(target), device_id_type=MESH,
-        )
-
-    def give(q, k):
-        i = q * 4 + k
-        source = chip_of(q, k)
-        return pltpu.make_async_remote_copy(
-            block(source, h), block(source, h), give_send.at[i], give_recv.at[i],
-            device_id=partner, device_id_type=MESH,
-        )
-
+            ref, ref, sems[0].at[i], sems[1].at[i], device_id=target, device_id_type=MESH
+        )
+
+    over_links, over_cores = (gather_send, gather_recv), (give_send, give_recv)
     started = []
-    for k in (1, 3, 2):
-        c = gather(0, k, ((z + k) % 4) * 4 + p, g)
+    gives = []
+
+    def send(q, k, cut, chip, target):
+        c = move(over_links, q, k, cut, chip, h, peer(target))
         c.start()
         started.append(c)
-    for q in (1, 3, 2):
-        c = gather(q, 0, z * 4 + (p + 4 - q) % 4, g)
+
+    def arrived(q, k, cut):
+        chip = chip_of(q, k)
+        move(over_links, q, k, cut, chip, h, partner).wait_recv()
+        c = move(over_cores, q, k, cut, chip, h, partner)
         c.start()
-        started.append(c)
-    gives = []
-
-    def arrived(q, k):
-        i = q * 4 + k
-        source = chip_of(q, k)
-        pltpu.make_async_remote_copy(
-            block(source, h), block(source, h), gather_send.at[i], gather_recv.at[i],
-            device_id=partner, device_id_type=MESH,
-        ).wait_recv()
-        c = give(q, k)
-        c.start()
-        gives.append((c, q, k))
+        gives.append((c, q, k, cut))
+
+    def forward_whole(k):
+        send(1, k, 0, chip_of(0, k), z * 4 + along_x)
+        send(2, k, 0, chip_of(0, k), z * 4 + along_y)
+
+    def forward_halves(k):
+        arrived(1, k, 0)
+        send(3, k, 2, chip_of(1, k), z * 4 + along_y)
+        arrived(2, k, 0)
+        send(3, k, 1, chip_of(2, k), z * 4 + along_x)
 
     for k in (1, 3, 2):
-        arrived(0, k)
-        for q in (1, 3, 2):
-            c = gather(q, k, z * 4 + (p + 4 - q) % 4, chip_of(0, k))
-            c.start()
-            started.append(c)
+        send(0, k, 0, g, ((z + k) % 4) * 4 + p)
+    forward_whole(0)
+    arrived(0, 1, 0)
+    forward_whole(1)
+    forward_halves(0)
+    arrived(0, 3, 0)
+    forward_whole(3)
+    forward_halves(1)
+    arrived(0, 2, 0)
+    forward_whole(2)
+    forward_halves(3)
+    forward_halves(2)
     for k in (0, 1, 3, 2):
-        for q in (1, 3, 2):
-            arrived(q, k)
-    for c, q, k in gives:
-        i = q * 4 + k
-        theirs = block(chip_of(q, k), 1 - h)
-        pltpu.make_async_remote_copy(
-            theirs, theirs, give_send.at[i], give_recv.at[i], device_id=partner, device_id_type=MESH
-        ).wait_recv()
+        arrived(3, k, 1)
+        arrived(3, k, 2)
+    for c, q, k, cut in gives:
+        move(over_cores, q, k, cut, chip_of(q, k), 1 - h, partner).wait_recv()
     for c in started:
         c.wait_send()
-    for c, q, k in gives:
+    for c, q, k, cut in gives:
         c.wait_send()
 
     left = y_all[0, :, :half]
     right = y_all[1, :, :half]
     gram = mm(left, left, NT) + mm(right, right, NT)
-    old = y_all[0, :, half:][:, : fx_ref.shape[1]].astype(F32)
+    old = y_all[0, :, half:][:, :ra].astype(F32)
     power_x = mm(gram, old, NN, HIGH)
     inv_x = inverse_lower(mm(power_x, power_x, TN, HIGH))
     qx = mm(power_x, inv_x, NT, HIGH)
@@ -198,17 +221,47 @@
         both = jnp.concatenate([jnp.concatenate([hi, hi], 1), jnp.concatenate([lo, lo], 1)], 0)
         acc = acc + mm(both, pp_ref[x], NT)
     power_y = acc[:nb] + acc[nb:]
-    for i, flip in enumerate((1, 2, 4, 8)):
-        low = g % (2 * flip)
-        target = jnp.where(low < flip, g + flip, g - flip)
-        wy_send[i] = power_y
+    ny = power_y.shape[1]
+    wide = ny // 4
+    for c in range(chips):
+        wy_send[c, :, :wide] = power_y[c // 4 * 8 : c // 4 * 8 + 8, c % 4 * wide : (c % 4 + 1) * wide]
+        wy_send[c, :, wide:] = jnp.zeros((8, LANES - wide), F32)
+    sends = []
+    for k in range(1, chips):
+        target = (g + k) % chips
         c = pltpu.make_async_remote_copy(
-            wy_send.at[i], wy_recv.at[i], wy_sem.at[0, i], wy_sem.at[1, i],
+            wy_send.at[target], wy_recv.at[k], wy_sem.at[0, k], wy_sem.at[1, k],
             device_id=peer(target), device_id_type=MESH,
         )
         c.start()
-        c.wait()
-        power_y = power_y + wy_recv[i]
+        sends.append(c)
+    piece = wy_send[g]
+    for k, c in enumerate(sends):
+        c.wait_recv()
+        piece = piece + wy_recv[k + 1]
+    wy_all[g] = piece
+
+    def spread_piece(chip, k, target):
+        return pltpu.make_async_remote_copy(
+            wy_all.at[chip], wy_all.at[chip], wy_sem.at[2, k], wy_sem.at[3, k],
+            device_id=target, device_id_type=MESH,
+        )
+
+    for k in range(1, chips):
+        c = spread_piece(g, k, peer((g + k) % chips))
+        c.start()
+        sends.append(c)
+    for k in range(1, chips):
+        spread_piece((g + chips - k) % chips, k, partner).wait_recv()
+    for c in sends:
+        c.wait_send()
+    power_y = jnp.concatenate(
+        [
+            jnp.concatenate([wy_all[r * 4 + u][:, :wide] for u in range(4)], axis=1)
+            for r in range(nb // 8)
+        ],
+        axis=0,
+    )
 
     my_send[...] = jnp.zeros(my_send.shape, F32)
     my_send[:, :nb] = mm(power_y, power_y, NT, HIGH)
@@ -256,73 +309,52 @@
 
     my_copy.wait()
     inv_y = inverse_lower(my_send[:, :nb] + my_recv[:, :nb])
-    fy_out[...] = scale_y * mm(power_y, inv_y, (((0,), (1,)), ((), ())), HIGH)
+    fy_out[...] = scale_y * mm(inv_y, power_y, NN, HIGH)
 
     for cp in sends:
         cp.wait()
     total = mine[g]
     for k in range(1, chips):
         total = total + landed[k]
-    ra = fx_ref.shape[1]
     columns = [
         jnp.concatenate([total[i][:, u * ra : (u + 1) * ra] for u in range(nb // 8)], axis=0)
         for i in range(mine_rows)
     ]
     raw = jnp.concatenate(columns, axis=1)
-    core_out[...] = mm(raw, inv_y, (((0,), (1,)), ((), ())), HIGH)
+    core_out[...] = mm(inv_y, raw, NN, HIGH)
 
 
 def fast_body(chips, field, factor_x_old, factor_y_old, factor_z, factor_t):
     nt, nx, ny, nz = field.shape
     ra = factor_x_old.shape[1]
     nb = factor_y_old.shape[1]
-    nc = factor_z.shape[1]
-    nd = factor_t.shape[1]
-    fz = jnp.tile(factor_z.astype(F32), (1, nd))
-    ft = jnp.repeat(factor_t.astype(F32), nc, axis=1)
-    whole = lambda shape: pl.BlockSpec(shape, lambda x: (0,) * len(shape))
-    pp, a = pl.pallas_call(
-        project_kernel,
-        grid=(nx,),
-        in_specs=[
-            pl.BlockSpec((nt, 1, ny, nz), lambda x: (0, x, 0, 0)),
-            whole((nz, LANES)), whole((nt, LANES)), whole((ny, nb)),
-        ],
-        out_specs=[
-            pl.BlockSpec((1, ny, 2 * LANES), lambda x: (x, 0, 0)),
-            pl.BlockSpec((1, nb, LANES), lambda x: (x, 0, 0)),
-        ],
-        out_shape=[
-            jax.ShapeDtypeStruct((nx, ny, 2 * LANES), BF16),
-            jax.ShapeDtypeStruct((nx, nb, LANES), F32),
-        ],
-        scratch_shapes=[pltpu.VMEM((nt, nz, 2 * LANES), BF16), pltpu.VMEM((nb, ny), BF16)],
-        compiler_params=pltpu.CompilerParams(
-            dimension_semantics=("arbitrary",), vmem_limit_bytes=32 << 20
-        ),
-    )(field, fz, ft, factor_y_old)
     xs = nx * chips
     wide = nb * LANES
     rows = LANES // (2 * chips)
     vmem = pl.BlockSpec(memory_space=pltpu.VMEM)
     dma = pltpu.SemaphoreType.DMA
-    return pl.pallas_call(
+    factor_x, factor_y, core = pl.pallas_call(
         functools.partial(tucker_kernel, chips, math.sqrt(xs), math.sqrt(2 * ny)),
-        in_specs=[vmem] * 3,
+        in_specs=[pl.BlockSpec(memory_space=pl.ANY)] + [vmem] * 4,
         out_specs=[vmem] * 3,
         out_shape=[
             jax.ShapeDtypeStruct((nx, ra), F32),
-            jax.ShapeDtypeStruct((ny, nb), F32),
-            jax.ShapeDtypeStruct((rows * ra, nb), F32),
+            jax.ShapeDtypeStruct((nb, ny), F32),
+            jax.ShapeDtypeStruct((nb, rows * ra), F32),
         ],
         scratch_shapes=[
+            pltpu.VMEM((3, nt, 2, ny, nz), BF16),
+            pltpu.VMEM((nt, nz, 2 * LANES), BF16),
+            pltpu.VMEM((nx, ny, 2 * LANES), BF16),
+            pltpu.VMEM((nx, nb, LANES), F32),
             pltpu.VMEM((nx, wide), F32),
             pltpu.VMEM((nx, wide), F32),
             pltpu.VMEM((2, xs, wide // 2 + LANES), BF16),
             pltpu.VMEM((xs, ra), F32),
             pltpu.VMEM((nb, nx, LANES), F32),
-            pltpu.VMEM((4, nb, ny), F32),
-            pltpu.VMEM((4, nb, ny), F32),
+            pltpu.VMEM((chips, 8, LANES), F32),
+            pltpu.VMEM((chips, 8, LANES), F32),
+            pltpu.VMEM((chips, 8, LANES), F32),
             pltpu.VMEM((nb, LANES), F32),
             pltpu.VMEM((nb, LANES), F32),
             pltpu.VMEM((nx, nb, LANES), F32),
@@ -331,12 +363,13 @@
             pltpu.VMEM((chips, rows, 8, LANES), F32),
             pltpu.VMEM((chips, rows, 8, LANES), F32),
             pltpu.VMEM((chips, rows, 8, LANES), F32),
-            dma((4,)), dma((16,)), dma((16,)), dma((16,)), dma((16,)), dma((2, 4)), dma((2, chips)), dma((2, chips)),
+            dma((3,)), dma((4,)), dma((24,)), dma((24,)), dma((24,)), dma((24,)), dma((4, chips)), dma((2, chips)), dma((2, chips)),
         ],
         compiler_params=pltpu.CompilerParams(
-            collective_id=0, has_side_effects=True, vmem_limit_bytes=40 << 20
+            collective_id=0, has_side_effects=True, vmem_limit_bytes=52 << 20
         ),
-    )(pp, a, factor_x_old)
+    )(field, factor_x_old, factor_y_old.T, factor_z.T, factor_t.T)
+    return factor_x, factor_y.T, core.T
 
 
 def orthonormal(power, gram):
@@ -410,7 +443,7 @@
             and field.shape[1] == 16
             and factor_x_old.shape[1] == 32
             and factor_y_old.shape[1] == 32
-            and field.shape[2] % 256 == 0
+            and field.shape[2] == 256
             and field.shape[3] % 256 == 0
         )
         if fits:

time: 76.4 us -> 69.5 us (0.910)
  local copies, waits for them, and re-layouts: 10.3 us -> 4.61 us
  Pallas kernels: 65.1 us -> 63.4 us
    pallas_call x1 -> x0, Pallas kernels: 11.1 us -> none  [fast_body(): pl.pallas_call(project_kernel, grid=(nx,), in_specs=[pl.BlockSpec((nt, 1,...]
    pallas_call x1, Pallas kernels: 54 us -> 63.4 us  [fast_body(): pl.pallas_call(functools.partial(tucker_kernel, chips, math.sqrt(xs), mat...]
    unnamed x6 -> x11, local copies, waits for them, and re-layouts: 7.21 us -> 4.61 us
    pallas_call x2 -> x0, local copies, waits for them, and re-layouts: 1.37 us -> none  [fast_body(): pl.pallas_call(functools.partial(tucker_kernel, chips, math.sqrt(xs), mat...]
    another operation x2 -> x0, local copies, waits for them, and re-layouts: 0.82 us -> none  [fast_body(): fz = jnp.tile(factor_z.astype(F32), (1, nd))]
    convert_element_type x1 -> x0, local copies, waits for them, and re-layouts: 0.77 us -> none  [fast_body(): ft = jnp.repeat(factor_t.astype(F32), nc, axis=1)]
where the time goes in v2:
time: 69.5 us; the launch traced here: 68.6 us
  Pallas kernels  63.4 us (91%)
  local copies, waits for them, and re-layouts  4.61 us (7%)
    pallas_call x1, Pallas kernels, fast_body(): pl.pallas_call(functools.partial(tucker_kernel, chips, math.sqrt(xs), mat...  63.4 us
    unnamed x11, local copies, waits for them, and re-layouts  4.61 us

profile of v2, /device:TPU:0, one launch (start us, length us, event | category | flops | bytes accessed | tf_op | source)
XLA Modules:
  0.0 68.6 jit_solution(2516171538896805777)
XLA Ops:
  0.6 0.0 copy-start
  0.6 0.7 %copy-done = bf16[256,32]{0,1:T(8,128)(2,1)S(1)} copy-done((bf16[256,32]{0,1:T(8,128)(2,1)S(1)}, bf16[256,32]{0,1:T(8,128)(2,1)}, u32[]{:S(2)}) %copy-start) | copy-done | bytes 16408
  1.4 0.0 copy-start.1
  1.4 0.7 %copy-done.1 = bf16[256,32]{0,1:T(8,128)(2,1)S(1)} copy-done((bf16[256,32]{0,1:T(8,128)(2,1)S(1)}, bf16[256,32]{0,1:T(8,128)(2,1)}, u32[]{:S(2)}) %copy-start.1) | copy-done | bytes 16408
  2.1 0.0 copy-start.2
  2.1 0.7 copy-done.2
  2.8 0.0 copy-start.3
  2.8 0.7 copy-done.3
  3.4 63.4 %shard_map.76 = (f32[16,32]{1,0:T(8,128)S(1)}, f32[32,256]{1,0:T(8,128)S(1)}, f32[32,128]{1,0:T(8,128)S(1)}) custom-call(bf16[8,16,256,256]{3,2,1,0:T(8,128)(2,1)} %field_ref.1, bf16[16,32]{1,0:T(8,128)(2,1)S(1)} %copy-done.2, bf16[32,256]{1,0:T(8,128)(2,1)S(1)} %bitcast.6, bf16[32,256]{1,0:T(8,128)(2,1)S(1)} %bitcast.7, bf16[4,8]{1,0:T(4,128)(2,1)S(1)} %bitcast.9), custom_call_target="tpu_custom_call" | custom-call | tf_op jit(solution)/shard_map/pallas_call | solution.py:336
  66.8 0.6 copy.11
  67.4 0.6 copy.12
  68.0 0.6 copy.13
Async XLA Ops:
  0.6 0.7 %copy-start = (bf16[256,32]{0,1:T(8,128)(2,1)S(1)}, bf16[256,32]{0,1:T(8,128)(2,1)}, u32[]{:S(2)}) copy-start(bf16[256,32]{0,1:T(8,128)(2,1)} %param.7) | copy-start | bytes 49156
  1.4 0.7 %copy-start.1 = (bf16[256,32]{0,1:T(8,128)(2,1)S(1)}, bf16[256,32]{0,1:T(8,128)(2,1)}, u32[]{:S(2)}) copy-start(bf16[256,32]{0,1:T(8,128)(2,1)} %param.8) | copy-start | bytes 49156
  2.1 0.7 %copy-start.2 = (bf16[16,32]{1,0:T(8,128)(2,1)S(1)}, bf16[16,32]{1,0:T(8,128)(2,1)}, u32[]{:S(2)}) copy-start(bf16[16,32]{1,0:T(8,128)(2,1)} %fx_ref.1) | copy-start | bytes 3076
  2.8 0.7 copy-start.3

commit v3 on v1

--- a/solution.py
+++ b/solution.py
@@ -49,52 +49,81 @@
     return both[:, n:] * lax.rsqrt(diag)
 
 
-def project_kernel(field_ref, fz_ref, ft_ref, fy_ref, pp_ref, a_ref, w_ref, fyt_ref):
-    steps = field_ref.shape[0]
-
-    @pl.when(pl.program_id(0) == 0)
-    def _():
-        for t in range(steps):
-            hi, lo = split2(fz_ref[...] * ft_ref[t : t + 1, :])
-            w_ref[t, :, :LANES] = hi
-            w_ref[t, :, LANES:] = lo
-        fyt_ref[...] = fy_ref[...].astype(F32).T.astype(BF16)
-
-    acc = mm(field_ref[0, 0], w_ref[0], NN)
-    for t in range(1, steps):
-        acc = acc + mm(field_ref[t, 0], w_ref[t], NN)
-    hi, lo = split2(acc[:, :LANES] + acc[:, LANES:])
-    pp = jnp.concatenate([hi, lo], axis=1)
-    pp_ref[0] = pp
-    rows = mm(fyt_ref[...], pp, NN)
-    a_ref[0] = rows[:, :LANES] + rows[:, LANES:]
-
-
 def tucker_kernel(
     chips, scale_x, scale_y,
-    pp_ref, a_ref, fx_ref,
+    field_ref, fx_in, fyt_in, fzt_in, ftt_in,
     fx_out, fy_out, core_out,
-    part, other, y_all, qx_ref, s3, wy_send, wy_recv, my_send, my_recv, fold, fold2, shares, pair_in, mine, landed,
-    pair_sem, gather_send, gather_recv, give_send, give_recv, wy_sem, core_send, core_recv,
+    fx_ref, fyt_ref, fzt_ref, ftt_ref, slots, w_ref, pp_ref, a_ref,
+    part, other, y_all, qx_ref, s3, wy_all, my_send, my_recv, fold, fold2, shares, pair_in, mine, landed,
+    field_sem, pair_sem, gather_send, gather_recv, give_send, give_recv, wy_sem, core_send, core_recv, small_sem,
 ):
     grp = lax.axis_index("grp")
     g = lax.axis_index("gx")
     h = lax.axis_index("gy")
     z = g // 4
     p = g % 4
-    nx = a_ref.shape[0]
-    nb = a_ref.shape[1]
+    depth, pair = slots.shape[0], slots.shape[2]
+    nt, nx = field_ref.shape[:2]
+    nb, ra, nd = fyt_ref.shape[0], fx_ref.shape[1], ftt_ref.shape[0]
+    nc = fzt_ref.shape[0]
     half = nb // 2 * LANES
-    xs = chips * nx
     partner = (grp, g, 1 - h)
 
     def peer(chip):
         return (grp, chip, h)
+
+    def fetch(i):
+        slot = lax.rem(i, depth)
+        return pltpu.make_async_copy(
+            field_ref.at[:, pl.ds(i * pair, pair)], slots.at[slot], field_sem.at[slot]
+        )
+
+    small = [
+        pltpu.make_async_copy(src, dst, small_sem.at[i])
+        for i, (src, dst) in enumerate(
+            ((fzt_in, fzt_ref), (ftt_in, ftt_ref), (fyt_in, fyt_ref), (fx_in, fx_ref))
+        )
+    ]
+    for c in small:
+        c.start()
+    steps = nx // pair
+    for i in range(depth - 1):
+        fetch(i).start()
 
     barrier = pltpu.get_barrier_semaphore()
     pl.semaphore_signal(barrier, inc=1, device_id=partner, device_id_type=MESH)
     for k in range(1, chips):
         pl.semaphore_signal(barrier, inc=1, device_id=peer((g + k) % chips), device_id_type=MESH)
+
+    for c in small:
+        c.wait()
+
+    ftt = ftt_ref[...].astype(F32)
+    fz = jnp.concatenate([fzt_ref[...].astype(F32)] * nd, axis=0).T
+    ft = jnp.concatenate([jnp.broadcast_to(ftt[d : d + 1, :], (nc, nt)) for d in range(nd)], axis=0).T
+    for t in range(nt):
+        hi, lo = split2(fz * ft[t : t + 1, :])
+        w_ref[t, :, :LANES] = hi
+        w_ref[t, :, LANES:] = lo
+
+    @pl.loop(0, steps)
+    def _(i):
+        @pl.when(i + depth - 1 < steps)
+        def _():
+            fetch(i + depth - 1).start()
+
+        fetch(i).wait()
+        slot = lax.rem(i, depth)
+        for u in range(pair):
+            acc = mm(slots[slot, 0, u], w_ref[0], NN)
+            for t in range(1, nt):
+                acc = acc + mm(slots[slot, t, u], w_ref[t], NN)
+            hi, lo = split2(acc[:, :LANES] + acc[:, LANES:])
+            pp = jnp.concatenate([hi, lo], axis=1)
+            pp_ref[i * pair + u] = pp
+            rows = mm(fyt_ref[...], pp, NN)
+            a_ref[i * pair + u] = rows[:, :LANES] + rows[:, LANES:]
+
     for b in range(nb):
         part[:, b * LANES : (b + 1) * LANES] = a_ref[:, b, :]
     pl.semaphore_wait(barrier, chips)
@@ -106,7 +135,7 @@
     own = pl.ds(pl.multiple_of(g * nx, nx), nx)
     for s in range(2):
         y_all[s, own, half:] = jnp.zeros((nx, LANES), BF16)
-        y_all[s, own, half : half + fx_ref.shape[1]] = fx_ref[...]
+        y_all[s, own, half : half + ra] = fx_ref[...]
     swap.wait()
     for s in range(2):
         at = slice(s * half, (s + 1) * half)
@@ -178,7 +207,7 @@
     left = y_all[0, :, :half]
     right = y_all[1, :, :half]
     gram = mm(left, left, NT) + mm(right, right, NT)
-    old = y_all[0, :, half:][:, : fx_ref.shape[1]].astype(F32)
+    old = y_all[0, :, half:][:, :ra].astype(F32)
     power_x = mm(gram, old, NN, HIGH)
     inv_x = inverse_lower(mm(power_x, power_x, TN, HIGH))
     qx = mm(power_x, inv_x, NT, HIGH)
@@ -198,17 +227,27 @@
         both = jnp.concatenate([jnp.concatenate([hi, hi], 1), jnp.concatenate([lo, lo], 1)], 0)
         acc = acc + mm(both, pp_ref[x], NT)
     power_y = acc[:nb] + acc[nb:]
-    for i, flip in enumerate((1, 2, 4, 8)):
-        low = g % (2 * flip)
-        target = jnp.where(low < flip, g + flip, g - flip)
-        wy_send[i] = power_y
-        c = pltpu.make_async_remote_copy(
-            wy_send.at[i], wy_recv.at[i], wy_sem.at[0, i], wy_sem.at[1, i],
-            device_id=peer(target), device_id_type=MESH,
-        )
-        c.start()
-        c.wait()
-        power_y = power_y + wy_recv[i]
+    sends = []
+    for phase, at in ((0, p), (1, z)):
+        wy_all[phase, at] = power_y
+
+        def exchange(k, target, source):
+            ref = wy_all.at[phase, source]
+            return pltpu.make_async_remote_copy(
+                ref, ref, wy_sem.at[2 * phase, k], wy_sem.at[2 * phase + 1, k],
+                device_id=target, device_id_type=MESH,
+            )
+
+        for k in (1, 3, 2):
+            to = (at + k) % 4
+            c = exchange(k, peer(z * 4 + to if phase == 0 else to * 4 + p), at)
+            c.start()
+            sends.append(c)
+        for k in (1, 3, 2):
+            exchange(k, partner, (at + 4 - k) % 4).wait_recv()
+        power_y = (wy_all[phase, 0] + wy_all[phase, 1]) + (wy_all[phase, 2] + wy_all[phase, 3])
+    for c in sends:
+        c.wait_send()
 
     my_send[...] = jnp.zeros(my_send.shape, F32)
     my_send[:, :nb] = mm(power_y, power_y, NT, HIGH)
@@ -256,73 +295,54 @@
 
     my_copy.wait()
     inv_y = inverse_lower(my_send[:, :nb] + my_recv[:, :nb])
-    fy_out[...] = scale_y * mm(power_y, inv_y, (((0,), (1,)), ((), ())), HIGH)
+    fy_out[...] = scale_y * mm(inv_y, power_y, NN, HIGH)
 
     for cp in sends:
         cp.wait()
     total = mine[g]
     for k in range(1, chips):
         total = total + landed[k]
-    ra = fx_ref.shape[1]
     columns = [
         jnp.concatenate([total[i][:, u * ra : (u + 1) * ra] for u in range(nb // 8)], axis=0)
         for i in range(mine_rows)
     ]
     raw = jnp.concatenate(columns, axis=1)
-    core_out[...] = mm(raw, inv_y, (((0,), (1,)), ((), ())), HIGH)
+    core_out[...] = mm(inv_y, raw, NN, HIGH)
 
 
 def fast_body(chips, field, factor_x_old, factor_y_old, factor_z, factor_t):
     nt, nx, ny, nz = field.shape
     ra = factor_x_old.shape[1]
     nb = factor_y_old.shape[1]
-    nc = factor_z.shape[1]
-    nd = factor_t.shape[1]
-    fz = jnp.tile(factor_z.astype(F32), (1, nd))
-    ft = jnp.repeat(factor_t.astype(F32), nc, axis=1)
-    whole = lambda shape: pl.BlockSpec(shape, lambda x: (0,) * len(shape))
-    pp, a = pl.pallas_call(
-        project_kernel,
-        grid=(nx,),
-        in_specs=[
-            pl.BlockSpec((nt, 1, ny, nz), lambda x: (0, x, 0, 0)),
-            whole((nz, LANES)), whole((nt, LANES)), whole((ny, nb)),
-        ],
-        out_specs=[
-            pl.BlockSpec((1, ny, 2 * LANES), lambda x: (x, 0, 0)),
-            pl.BlockSpec((1, nb, LANES), lambda x: (x, 0, 0)),
-        ],
-        out_shape=[
-            jax.ShapeDtypeStruct((nx, ny, 2 * LANES), BF16),
-            jax.ShapeDtypeStruct((nx, nb, LANES), F32),
-        ],
-        scratch_shapes=[pltpu.VMEM((nt, nz, 2 * LANES), BF16), pltpu.VMEM((nb, ny), BF16)],
-        compiler_params=pltpu.CompilerParams(
-            dimension_semantics=("arbitrary",), vmem_limit_bytes=32 << 20
-        ),
-    )(field, fz, ft, factor_y_old)
     xs = nx * chips
     wide = nb * LANES
     rows = LANES // (2 * chips)
     vmem = pl.BlockSpec(memory_space=pltpu.VMEM)
     dma = pltpu.SemaphoreType.DMA
-    return pl.pallas_call(
+    factor_x, factor_y, core = pl.pallas_call(
         functools.partial(tucker_kernel, chips, math.sqrt(xs), math.sqrt(2 * ny)),
-        in_specs=[vmem] * 3,
+        in_specs=[pl.BlockSpec(memory_space=pltpu.HBM)] * 5,
         out_specs=[vmem] * 3,
         out_shape=[
             jax.ShapeDtypeStruct((nx, ra), F32),
-            jax.ShapeDtypeStruct((ny, nb), F32),
-            jax.ShapeDtypeStruct((rows * ra, nb), F32),
+            jax.ShapeDtypeStruct((nb, ny), F32),
+            jax.ShapeDtypeStruct((nb, rows * ra), F32),
         ],
         scratch_shapes=[
+            pltpu.VMEM((nx, ra), BF16),
+            pltpu.VMEM((nb, ny), BF16),
+            pltpu.VMEM(factor_z.shape[::-1], BF16),
+            pltpu.VMEM(factor_t.shape[::-1], BF16),
+            pltpu.VMEM((5, nt, 2, ny, nz), BF16),
+            pltpu.VMEM((nt, nz, 2 * LANES), BF16),
+            pltpu.VMEM((nx, ny, 2 * LANES), BF16),
+            pltpu.VMEM((nx, nb, LANES), F32),
             pltpu.VMEM((nx, wide), F32),
             pltpu.VMEM((nx, wide), F32),
             pltpu.VMEM((2, xs, wide // 2 + LANES), BF16),
             pltpu.VMEM((xs, ra), F32),
             pltpu.VMEM((nb, nx, LANES), F32),
-            pltpu.VMEM((4, nb, ny), F32),
-            pltpu.VMEM((4, nb, ny), F32),
+            pltpu.VMEM((2, 4, nb, ny), F32),
             pltpu.VMEM((nb, LANES), F32),
             pltpu.VMEM((nb, LANES), F32),
             pltpu.VMEM((nx, nb, LANES), F32),
@@ -331,12 +351,13 @@
             pltpu.VMEM((chips, rows, 8, LANES), F32),
             pltpu.VMEM((chips, rows, 8, LANES), F32),
             pltpu.VMEM((chips, rows, 8, LANES), F32),
-            dma((4,)), dma((16,)), dma((16,)), dma((16,)), dma((16,)), dma((2, 4)), dma((2, chips)), dma((2, chips)),
+            dma((5,)), dma((4,)), dma((16,)), dma((16,)), dma((16,)), dma((16,)), dma((4, 4)), dma((2, chips)), dma((2, chips)), dma((4,)),
         ],
         compiler_params=pltpu.CompilerParams(
-            collective_id=0, has_side_effects=True, vmem_limit_bytes=40 << 20
+            collective_id=0, has_side_effects=True, vmem_limit_bytes=52 << 20
         ),
-    )(pp, a, factor_x_old)
+    )(field, factor_x_old, factor_y_old.T, factor_z.T, factor_t.T)
+    return factor_x, factor_y.T, core.T
 
 
 def orthonormal(power, gram):
@@ -410,7 +431,7 @@
             and field.shape[1] == 16
             and factor_x_old.shape[1] == 32
             and factor_y_old.shape[1] == 32
-            and field.shape[2] % 256 == 0
+            and field.shape[2] == 256
             and field.shape[3] % 256 == 0
         )
         if fits:

time: 76.4 us -> 68.5 us (0.90)
  local copies, waits for them, and re-layouts: 10.3 us -> 4.61 us
  Pallas kernels: 65.1 us -> 62.8 us
    pallas_call x1 -> x0, Pallas kernels: 11.1 us -> none  [fast_body(): pl.pallas_call(project_kernel, grid=(nx,), in_specs=[pl.BlockSpec((nt, 1,...]
    pallas_call x1, Pallas kernels: 54 us -> 62.8 us  [fast_body(): pl.pallas_call(functools.partial(tucker_kernel, chips, math.sqrt(xs), mat...]
    unnamed x6 -> x11, local copies, waits for them, and re-layouts: 7.21 us -> 4.61 us
    pallas_call x2 -> x0, local copies, waits for them, and re-layouts: 1.37 us -> none  [fast_body(): pl.pallas_call(functools.partial(tucker_kernel, chips, math.sqrt(xs), mat...]
    another operation x2 -> x0, local copies, waits for them, and re-layouts: 0.82 us -> none  [fast_body(): fz = jnp.tile(factor_z.astype(F32), (1, nd))]
    convert_element_type x1 -> x0, local copies, waits for them, and re-layouts: 0.77 us -> none  [fast_body(): ft = jnp.repeat(factor_t.astype(F32), nc, axis=1)]
where the time goes in v3:
time: 68.5 us; the launch traced here: 68.1 us
  Pallas kernels  62.8 us (92%)
  local copies, waits for them, and re-layouts  4.61 us (7%)
    pallas_call x1, Pallas kernels, fast_body(): pl.pallas_call(functools.partial(tucker_kernel, chips, math.sqrt(xs), mat...  62.8 us
    unnamed x11, local copies, waits for them, and re-layouts  4.61 us

profile of v3, /device:TPU:0, one launch (start us, length us, event | category | flops | bytes accessed | tf_op | source)
XLA Modules:
  0.0 68.1 jit_solution(11669222238051700828)
XLA Ops:
  0.6 0.0 copy-start
  0.6 0.7 %copy-done = bf16[256,32]{0,1:T(8,128)(2,1)S(1)} copy-done((bf16[256,32]{0,1:T(8,128)(2,1)S(1)}, bf16[256,32]{0,1:T(8,128)(2,1)}, u32[]{:S(2)}) %copy-start) | copy-done | bytes 16408
  1.4 0.0 copy-start.1
  1.4 0.7 %copy-done.1 = bf16[256,32]{0,1:T(8,128)(2,1)S(1)} copy-done((bf16[256,32]{0,1:T(8,128)(2,1)S(1)}, bf16[256,32]{0,1:T(8,128)(2,1)}, u32[]{:S(2)}) %copy-start.1) | copy-done | bytes 16408
  2.1 0.0 copy-start.2
  2.1 0.7 %copy-done.2 = bf16[16,32]{1,0:T(8,128)(2,1)S(1)} copy-done((bf16[16,32]{1,0:T(8,128)(2,1)S(1)}, bf16[16,32]{1,0:T(8,128)(2,1)}, u32[]{:S(2)}) %copy-start.2) | copy-done | bytes 1048
  2.8 0.0 copy-start.3
  2.8 0.7 copy-done.3
  3.4 62.8 %shard_map.76 = (f32[16,32]{1,0:T(8,128)S(1)}, f32[32,256]{1,0:T(8,128)S(1)}, f32[32,128]{1,0:T(8,128)S(1)}) custom-call(bf16[8,16,256,256]{3,2,1,0:T(8,128)(2,1)} %field_ref.1, bf16[16,32]{1,0:T(8,128)(2,1)S(1)} %copy-done.2, bf16[32,256]{1,0:T(8,128)(2,1)S(1)} %bitcast.6, bf16[32,256]{1,0:T(8,128)(2,1)S(1)} %bitcast.7, bf16[4,8]{1,0:T(4,128)(2,1)S(1)} %bitcast.9), custom_call_target="tpu_custom_call" | custom-call | tf_op jit(solution)/shard_map/pallas_call | solution.py:322
  66.3 0.6 copy.11
  66.9 0.6 copy.12
  67.5 0.6 copy.13
Async XLA Ops:
  0.6 0.7 %copy-start = (bf16[256,32]{0,1:T(8,128)(2,1)S(1)}, bf16[256,32]{0,1:T(8,128)(2,1)}, u32[]{:S(2)}) copy-start(bf16[256,32]{0,1:T(8,128)(2,1)} %param.7) | copy-start | bytes 49156
  1.4 0.7 %copy-start.1 = (bf16[256,32]{0,1:T(8,128)(2,1)S(1)}, bf16[256,32]{0,1:T(8,128)(2,1)}, u32[]{:S(2)}) copy-start(bf16[256,32]{0,1:T(8,128)(2,1)} %param.8) | copy-start | bytes 49156
  2.1 0.7 %copy-start.2 = (bf16[16,32]{1,0:T(8,128)(2,1)S(1)}, bf16[16,32]{1,0:T(8,128)(2,1)}, u32[]{:S(2)}) copy-start(bf16[16,32]{1,0:T(8,128)(2,1)} %fx_in.1) | copy-start | bytes 3076
  2.8 0.7 copy-start.3

commit v4 on v3

--- a/solution.py
+++ b/solution.py
@@ -308,6 +308,12 @@
     ]
     raw = jnp.concatenate(columns, axis=1)
     core_out[...] = mm(inv_y, raw, NN, HIGH)
+
+
+def finish_kernel(fx_ref, fy_ref, core_ref, fx_out, fy_out, core_out):
+    fx_out[...] = fx_ref[...]
+    fy_out[...] = fy_ref[...]
+    core_out[...] = core_ref[...]
 
 
 def fast_body(chips, field, factor_x_old, factor_y_old, factor_z, factor_t):
@@ -357,6 +363,13 @@
             collective_id=0, has_side_effects=True, vmem_limit_bytes=52 << 20
         ),
     )(field, factor_x_old, factor_y_old.T, factor_z.T, factor_t.T)
+    made = (factor_x, factor_y, core)
+    factor_x, factor_y, core = pl.pallas_call(
+        finish_kernel,
+        in_specs=[vmem] * 3,
+        out_specs=[vmem] * 3,
+        out_shape=[jax.ShapeDtypeStruct(v.shape, F32) for v in made],
+    )(*made)
     return factor_x, factor_y.T, core.T
 
 

time: 68.5 us -> 69.8 us (1.019)
  Pallas kernels: 62.8 us -> 64.2 us
    pallas_call x0 -> x1, Pallas kernels: none -> 1.38 us  [fast_body(): pl.pallas_call(finish_kernel, in_specs=[vmem] * 3, out_specs=[vmem] * 3,...]
    unnamed x11 -> x14, local copies, waits for them, and re-layouts: 4.61 us -> 4.59 us
where the time goes in v4:
time: 69.8 us; the launch traced here: 69.5 us
  Pallas kernels  64.2 us (92%)
  local copies, waits for them, and re-layouts  4.59 us (7%)
    pallas_call x1, Pallas kernels, fast_body(): pl.pallas_call(functools.partial(tucker_kernel, chips, math.sqrt(xs), mat...  62.8 us
    unnamed x14, local copies, waits for them, and re-layouts  4.59 us

profile of v4, /device:TPU:0, one launch (start us, length us, event | category | flops | bytes accessed | tf_op | source)
XLA Modules:
  0.0 69.5 jit_solution(18334225279577184594)
XLA Ops:
  0.6 0.0 copy-start.1
  0.6 0.7 %copy-done.1 = bf16[256,32]{0,1:T(8,128)(2,1)S(1)} copy-done((bf16[256,32]{0,1:T(8,128)(2,1)S(1)}, bf16[256,32]{0,1:T(8,128)(2,1)}, u32[]{:S(2)}) %copy-start.1) | copy-done | bytes 16408
  1.4 0.0 copy-start.2
  1.4 0.7 %copy-done.2 = bf16[256,32]{0,1:T(8,128)(2,1)S(1)} copy-done((bf16[256,32]{0,1:T(8,128)(2,1)S(1)}, bf16[256,32]{0,1:T(8,128)(2,1)}, u32[]{:S(2)}) %copy-start.2) | copy-done | bytes 16408
  2.1 0.0 copy-start.5
  2.1 0.7 copy-done.5
  2.8 0.0 copy-start.6
  2.8 0.7 copy-done.6
  3.4 62.8 %shard_map.76 = (f32[16,32]{1,0:T(8,128)S(1)}, f32[32,256]{1,0:T(8,128)S(1)}, f32[32,128]{1,0:T(8,128)S(1)}) custom-call(bf16[8,16,256,256]{3,2,1,0:T(8,128)(2,1)} %field_ref.1, bf16[16,32]{1,0:T(8,128)(2,1)S(1)} %copy-done.5, bf16[32,256]{1,0:T(8,128)(2,1)S(1)} %bitcast.5, bf16[32,256]{1,0:T(8,128)(2,1)S(1)} %bitcast.6, bf16[4,8]{1,0:T(4,128)(2,1)S(1)} %bitcast.7), custom_call_target="tpu_custom_call" | custom-call | tf_op jit(solution)/shard_map/pallas_call | solution.py:328
  66.3 0.0 copy-start
  66.3 0.6 copy-done
  66.9 0.0 copy-start.3
  66.9 0.6 copy-done.3
  67.5 0.0 copy-start.4
  67.5 0.6 copy-done.4
  68.1 1.4 %shard_map.77 = (f32[16,32]{1,0:T(8,128)}, f32[32,256]{1,0:T(8,128)}, f32[32,128]{1,0:T(8,128)}) custom-call(f32[16,32]{1,0:T(8,128)} %copy-done.4, f32[32,256]{1,0:T(8,128)} %copy-done, f32[32,128]{1,0:T(8,128)} %copy-done.3), custom_call_target="tpu_custom_call" | custom-call | tf_op jit(solution)/shard_map/pallas_call | solution.py:367
Async XLA Ops:
  0.6 0.7 %copy-start.1 = (bf16[256,32]{0,1:T(8,128)(2,1)S(1)}, bf16[256,32]{0,1:T(8,128)(2,1)}, u32[]{:S(2)}) copy-start(bf16[256,32]{0,1:T(8,128)(2,1)} %param.7) | copy-start | bytes 49156
  1.4 0.7 %copy-start.2 = (bf16[256,32]{0,1:T(8,128)(2,1)S(1)}, bf16[256,32]{0,1:T(8,128)(2,1)}, u32[]{:S(2)}) copy-start(bf16[256,32]{0,1:T(8,128)(2,1)} %param.8) | copy-start | bytes 49156
  2.1 0.7 copy-start.5
  2.8 0.7 copy-start.6
  66.3 0.6 copy-start
  66.9 0.6 copy-start.3
  67.5 0.6 copy-start.4
